TPU v7x, 32 devices: a whole 2x2x4 slice. The times are simulated.
32 devices in a mesh: groups: 2 (over y), fibre: 4 (over z), tm: 2 (over x), freq: 2 (over core).
Axes of the slice: x: 2, y: 2, z: 4, core: 2. Of those that a mesh axis runs over, the one named last changes fastest.
Arguments:
- strain_rate: bfloat16 [8, 512, 1024], P(('fibre', 'tm'), 'groups'), parts along dimension 1, may hold values from -40 to 40
Outputs:
- correlations: float32 [64, 512, 401], P(('tm', 'freq'), ('groups', 'fibre')), parts along dimension 1
There are 2 independent parts, one for each index of `groups`. A program takes and returns all parts, laid end to end along the dimension named above; each array names one. Nothing has to cross between parts.
All inputs are finite; a program needn't handle non-finite values.
Results may differ from a plain program's by a relative error of at most 0.0085.
Values may be sent and summed in bfloat16 or wider, within the bound.
A program may use at most 64 MiB of HBM per device.

v0:
```python
import math

import jax
import jax.numpy as jnp
from jax import lax
from jax.sharding import PartitionSpec as P

FREQS = 256
OFFS = 64
LAGS = 401


water_level = 0.5


def shifted(block, axis, distance):
    devices = range(lax.axis_size(axis))
    route = [(i - distance, i) for i in devices if i - distance in devices]
    return lax.ppermute(block, axis, route)


def forward_table(first_bin, bin_count, seg_length):
    sample_index = jnp.arange(seg_length, dtype=jnp.int32)
    bin_index = first_bin + jnp.arange(bin_count, dtype=jnp.int32)
    phase_index = sample_index[:, None] * bin_index[None, :] % seg_length
    angles = 2.0 * math.pi / seg_length * phase_index.astype(jnp.float32)
    hann_taper = 0.5 - 0.5 * jnp.cos(2.0 * math.pi / seg_length * sample_index.astype(jnp.float32))
    cosine = hann_taper[:, None] * jnp.cos(angles)
    sine_part = -hann_taper[:, None] * jnp.sin(angles)
    return jnp.concatenate([cosine, sine_part], axis=1).astype(jnp.bfloat16)


def inverse_table(first_bin, bin_count, lag_count, seg_length):
    bin_index = first_bin + jnp.arange(bin_count, dtype=jnp.int32)
    lag_index = jnp.arange(lag_count, dtype=jnp.int32) - (lag_count - 1) // 2
    phase_index = bin_index[:, None] * lag_index[None, :] % seg_length
    angles = 2.0 * math.pi / seg_length * phase_index.astype(jnp.float32)
    return jnp.concatenate([jnp.cos(angles), -jnp.sin(angles)], axis=0)


def whiten(spectra, band_power):
    water_floor = water_level * jnp.sqrt(band_power + 1e-06)
    amplitude = jnp.sqrt(spectra[:, :, 0] ** 2 + spectra[:, :, 1] ** 2)
    return (spectra / jnp.maximum(amplitude, water_floor[:, :, None])[:, :, None, :]).astype(
        jnp.bfloat16
    )


def local(strain_rate):
    local_bins = FREQS // lax.axis_size("freq")
    first_bin = 1 + lax.axis_index("freq") * local_bins
    seg_length = strain_rate.shape[2]
    blocks = lax.all_to_all(strain_rate, "fibre", split_axis=1, concat_axis=0, tiled=True)
    seg_count, chan_count, seg_length = blocks.shape
    spectra = jnp.dot(
        blocks.reshape(seg_count * chan_count, seg_length),
        forward_table(first_bin, local_bins, seg_length),
        preferred_element_type=jnp.float32,
    ).reshape(seg_count, chan_count, 2, local_bins)
    band_power = lax.psum(jnp.sum(spectra * spectra, axis=(2, 3)), "freq") / FREQS
    whitened = whiten(spectra, band_power)
    seg_count, chan_count = (whitened.shape[0], whitened.shape[1])
    neighbour = shifted(whitened, "fibre", -1)
    extended = jnp.concatenate([whitened, neighbour], axis=1)
    window = chan_count + OFFS
    own_layout = jnp.transpose(whitened, (3, 2, 0, 1))
    real_left = own_layout.reshape(local_bins, 2 * seg_count, chan_count)
    imag_left = jnp.concatenate([own_layout[:, 1], -own_layout[:, 0]], axis=1)
    left_side = jnp.stack([real_left, imag_left], axis=1)
    right_side = jnp.transpose(extended, (3, 2, 0, 1)).reshape(local_bins, 2 * seg_count, window)
    products = jnp.einsum(
        "brqc,bqm->brcm", left_side, right_side, preferred_element_type=jnp.float32
    )
    flat = products.reshape(local_bins, 2, chan_count * window)
    flat = jnp.pad(flat, ((0, 0), (0, 0), (0, chan_count)))
    skewed = flat.reshape(local_bins, 2, chan_count, window + 1)[:, :, :, 1 : OFFS + 1]
    group_sums = jnp.transpose(skewed, (3, 2, 1, 0))
    rounded = lax.optimization_barrier(group_sums.astype(jnp.bfloat16)).astype(jnp.float32)
    totals = lax.psum(rounded.astype(jnp.bfloat16), "tm").astype(jnp.float32)
    share = OFFS // lax.axis_size("tm")
    stacked = lax.dynamic_slice_in_dim(totals, lax.axis_index("tm") * share, share, 0)
    norm_factor = 1.0 / math.sqrt(seg_count * lax.axis_size("tm") * FREQS)
    terms = jnp.dot(
        stacked.reshape(-1, 2 * local_bins),
        inverse_table(first_bin, local_bins, LAGS, seg_length),
        precision=lax.Precision.HIGHEST,
        preferred_element_type=jnp.float32,
    )
    terms = terms.reshape(stacked.shape[0], chan_count, LAGS)
    correlations = lax.psum_scatter(
        terms.astype(jnp.bfloat16), "freq", scatter_dimension=0, tiled=True
    ).astype(jnp.float32)
    return correlations * norm_factor


def solution(mesh):
    placed = (P(("fibre", "tm"), "groups", None),)
    return jax.shard_map(
        local,
        mesh=mesh,
        in_specs=placed,
        out_specs=P(("tm", "freq"), ("groups", "fibre"), None),
        check_vma=False,
    )
```

profile of v0, /device:TPU:1, one launch (start us, length us, event | category | flops | bytes accessed | tf_op | source)
XLA Modules:
  0.0 161.9 jit_solution(2796082904154099239)
XLA Ops:
  6.5 1.9 %copy.40 = bf16[1,256,1024]{2,0,1:T(2,128)(2,1)S(1)} copy(bf16[1,256,1024]{2,1,0:T(8,128)(2,1)} %param.1) | data formatting | bytes 1048576 | tf_op args[0]
  8.4 0.5 broadcast.74
  8.9 3.7 %reduce.1 = bf16[256,1024]{1,0:T(8,128)(2,1)S(1)} reduce(bf16[256,1,1024]{2,1,0:T(2,128)(2,1)S(1)} %bitcast.39, bf16[]{:T(256)} %broadcast.74), dimensions={1}, to_apply=%bitcast.37.reduce_sub_computation | reduce | bytes 1048578
  12.6 1.2 reshape.59
  13.8 5.4 %all-to-all-start = ((bf16[4,2,32768]{2,1,0:T(2,128)(2,1)}), bf16[4,2,32768]{2,1,0:T(2,128)(2,1)S(1)}, u32[]{:S(2)}, u32[]{:S(2)}) async-start(bf16[4,2,32768]{2,1,0:T(2,128)(2,1)} %reshape.59), calls=%async_computation | async-start | bytes 1048576 | tf_op jit(solution)/shard_map/all_to_all | solution.py:53
  19.2 0.0 all-reduce.3.cloned.1.call-start
  19.3 2.3 %multiply_convert_fusion.1 = (bf16[1024,128]{1,0:T(8,128)(2,1)S(1)}, bf16[1024,128]{1,0:T(8,128)(2,1)S(1)}) fusion(s32[128]{0:T(128)S(1)} %iota_add_fusion.1, f32[1024]{0:T(1024)S(1)} %get-tuple-element.13, f32[1024]{0:T(1024)S(1)} %get-tuple-element.14), kind=kLoop, calls=%fused_computation.20 | loop fusion | flops 2359296 | bytes 532992 | tf_op jit(solution)/shard_map/convert.5
  21.5 11.7 %all-to-all-done = bf16[4,2,32768]{2,1,0:T(2,128)(2,1)S(1)} async-done(((bf16[4,2,32768]{2,1,0:T(2,128)(2,1)}), bf16[4,2,32768]{2,1,0:T(2,128)(2,1)S(1)}, u32[]{:S(2)}, u32[]{:S(2)}) %all-to-all-start) | async-done | bytes 524320 | tf_op jit(solution)/shard_map/all_to_all | solution.py:53
  33.2 0.5 reshape.60
  33.7 0.4 multiply_reduce_fusion
  34.1 0.1 copy.22
  34.3 0.1 reshape.53
  34.4 0.1 reduce_sum.12
  34.5 3.6 %psum.14 = f32[4,64]{1,0:T(4,128)S(1)} all-reduce(f32[4,64]{1,0:T(4,128)S(1)} %reduce_sum.12), channel_id=1, replica_groups=mesh['groups'=2,'fibre'=4,'tm'=2,'freq'=2] {'freq'}, use_global_device_ids=true, to_apply=%region_1.2 | all-reduce | flops 256 | bytes 2048 | tf_op jit(solution)/shard_map/psum | solution.py:60
  38.1 0.2 copy.24
  38.3 0.4 sqrt_maximum_fusion
  38.8 0.1 copy.23
  38.9 0.1 fusion.28
  39.1 0.1 divide_convert_fusion
  39.2 1.3 collective-permute-start
  40.5 0.1 slice_bitcast_fusion.1
  40.6 0.2 copy.25
  40.8 0.2 copy.26
  41.0 0.2 maximum_bitcast_fusion.2
  41.1 7.5 %collective-permute-done = bf16[4,64,2,128]{1,0,3,2:T(4,128)(2,1)S(1)} collective-permute-done((bf16[4,64,2,128]{1,0,3,2:T(4,128)(2,1)S(1)}, bf16[4,64,2,128]{1,0,3,2:T(4,128)(2,1)S(1)}, u32[]{:S(2)}, u32[]{:S(2)}) %collective-permute-start) | collective-permute-done | bytes 131104 | tf_op jit(solution)/shard_map/ppermute | solution.py:19
  48.6 0.4 maximum_bitcast_fusion.3
  49.0 0.1 copy.27
  49.1 3.3 %convolution_convert_fusion = bf16[128,2,64,128]{3,2,1,0:T(8,128)(2,1)} fusion(bf16[128,8,128,1]{2,1,3,0:T(8,128)(2,1)S(1)} %bitcast.40, bf16[128,1,8,64]{3,2,1,0:T(8,128)(2,1)S(1)} %maximum_bitcast_fusion.2, bf16[128,1,8,64]{3,2,1,0:T(8,128)(2,1)S(1)} %copy.26), kind=kOutput, calls=%fused_computation | convolution fusion | flops 35782656 | bytes 4718592 | tf_op jit(solution)/shard_map/brqc,bqm->brcm/dot_general | solution.py:71
  52.4 6.6 %copy.31 = bf16[128,2,64,128]{0,3,2,1:T(8,128)(2,1)} copy(bf16[128,2,64,128]{3,2,1,0:T(8,128)(2,1)} %convolution_convert_fusion) | data formatting | bytes 8388608 | tf_op jit(solution)/shard_map/reshape | solution.py:74
  59.0 3.8 %pad.5 = bf16[128,2,8256]{0,2,1:T(8,128)(2,1)} pad(bf16[128,2,8192]{0,2,1:T(8,128)(2,1)} %bitcast.38, bf16[]{:T(256)} %constant.55.clone.1), padding=0_0x0_0x0_64 | pad | bytes 8421378 | tf_op jit(solution)/shard_map/jit(_pad)/pad | solution.py:75
  62.8 7.1 %reshape.56 = bf16[128,2,64,129]{0,3,2,1:T(8,128)(2,1)} reshape(bf16[128,2,8256]{0,2,1:T(8,128)(2,1)} %pad.5) | data formatting | bytes 8454144 | tf_op jit(solution)/shard_map/reshape | solution.py:76
  69.9 4.1 %slice_bitcast_fusion = bf16[64,64,2,128]{3,0,1,2:T(8,128)(2,1)} fusion(bf16[128,2,64,129]{0,3,2,1:T(8,128)(2,1)} %reshape.56), kind=kLoop, calls=%fused_computation.1 | loop fusion | bytes 4194304 | tf_op jit(solution)/shard_map/convert_element_type | solution.py:78
  74.0 0.0 all-reduce.3.cloned.1.call-update
  74.0 0.2 reduce-scatter.2.cloned.1.call-start
  74.3 0.9 fusion.21
  75.2 60.6 %all-reduce.3.cloned.1.call-done = bf16[64,64,2,128]{3,0,1,2:T(8,128)(2,1)} async-done(((bf16[64,64,2,128]{3,0,1,2:T(8,128)(2,1)}), bf16[64,64,2,128]{3,0,1,2:T(8,128)(2,1)}) %all-reduce.3.cloned.1.call-update) | async-done | bytes 2097168 | tf_op jit(solution)/shard_map/psum | solution.py:79
  135.8 1.3 constant_dynamic-slice_fusion
  137.1 1.1 copy.29
  138.2 0.7 dot_general.16
  138.9 3.1 %convolution_convert_fusion.1 = bf16[32,64,401]{2,1,0:T(8,128)(2,1)} fusion(bf16[32,64,256]{2,1,0:T(8,128)(2,1)S(1)} %dot_general.16, f32[128,401]{0,1:T(8,128)S(1)} %get-tuple-element.8, f32[128,401]{0,1:T(8,128)S(1)} %get-tuple-element.7), kind=kOutput, calls=%fused_computation.3 | convolution fusion | flops 2523797760 | bytes 3101696 | tf_op jit(solution)/shard_map/dot_general | solution.py:83
  142.1 0.0 reduce-scatter.2.cloned.1.call-update
  142.1 10.1 %reduce-scatter.2.cloned.1.call-done = bf16[16,64,401]{2,1,0:T(8,128)(2,1)} async-done(((bf16[32,64,401]{2,1,0:T(8,128)(2,1)}), bf16[16,64,401]{2,1,0:T(8,128)(2,1)}) %reduce-scatter.2.cloned.1.call-update) | async-done | bytes 821264 | tf_op jit(solution)/shard_map/reduce_scatter | solution.py:90
  152.2 2.9 %convert_multiply_fusion = f32[16,64,401]{2,1,0:T(8,128)} fusion(bf16[16,64,401]{2,1,0:T(8,128)(2,1)} %reduce-scatter.2.cloned.1.call-done), kind=kLoop, calls=%fused_computation.2 | loop fusion | flops 821248 | bytes 2463744 | tf_op jit(solution)/shard_map/mul | solution.py:93
  (4 shorter events, 0.1 us)
Async XLA Ops:
  13.8 19.4 %all-to-all-start = ((bf16[4,2,32768]{2,1,0:T(2,128)(2,1)}), bf16[4,2,32768]{2,1,0:T(2,128)(2,1)S(1)}, u32[]{:S(2)}, u32[]{:S(2)}) async-start(bf16[4,2,32768]{2,1,0:T(2,128)(2,1)} %reshape.59), calls=%async_computation | async-start | bytes 1048576 | tf_op jit(solution)/shard_map/all_to_all | solution.py:53
  19.2 116.6 %all-reduce.3.cloned.1.call-start = ((), (), s32[]{:S(2)}) async-start(), calls=%async_computation.2 | async-start | bytes 4194304 | tf_op jit(solution)/shard_map/psum | solution.py:79
  39.2 9.4 %collective-permute-start = (bf16[4,64,2,128]{1,0,3,2:T(4,128)(2,1)S(1)}, bf16[4,64,2,128]{1,0,3,2:T(4,128)(2,1)S(1)}, u32[]{:S(2)}, u32[]{:S(2)}) collective-permute-start(bf16[4,64,2,128]{1,0,3,2:T(4,128)(2,1)S(1)} %divide_convert_fusion), channel_id=1, source_target_pairs={{4,0},{8,4},{12,8},{5,1},{9,5},{13,9},{6,2},{10,6},{14,10},{7,3},{... | collective-permute-start | bytes 393224 | tf_op jit(solution)/shard_map/ppermute | solution.py:19
  74.0 78.2 %reduce-scatter.2.cloned.1.call-start = ((), (), s32[]{:S(2)}) async-start(), calls=%async_computation.3 | async-start | bytes 3145728 | tf_op jit(solution)/shard_map/reduce_scatter | solution.py:90
Sparse Core Ops, SparseCore 0:
  74.1 61.6 all-reduce.2
  142.2 9.9 reduce-scatter.1
where the time goes:
time: 163 us; the launch traced here: 162 us
  waiting for transfers between devices  89.9 us (55%)
  local copies, waits for them, and re-layouts  29.9 us (18%)
  between operations  13.6 us (8%)
  other arithmetic  11.1 us (7%)
  starting transfers between devices  6.94 us (4%)
  matrix products  6.86 us (4%)
  blocking collectives  3.55 us (2%)
    psum x1, waiting for transfers between devices, local(): totals = lax.psum(rounded.astype(jnp.bfloat16), 'tm').astype(jnp.float32)  60.6 us
    all_to_all x1, waiting for transfers between devices, local(): lax.all_to_all(strain_rate, 'fibre', split_axis=1, concat_axis=0, tiled=T...  11.7 us
    reduce_scatter x1, waiting for transfers between devices, local(): lax.psum_scatter(terms.astype(jnp.bfloat16), 'freq', scatter_dimension=0,...  10.1 us
    ppermute x1, waiting for transfers between devices, shifted(): return lax.ppermute(block, axis, route)  7.49 us
    reshape x1, local copies, waits for them, and re-layouts, local(): flat.reshape(local_bins, 2, chan_count, window + 1)[:, :, :, 1:OFFS + 1]  7.12 us
    reshape x1, local copies, waits for them, and re-layouts, local(): flat = products.reshape(local_bins, 2, chan_count * window)  6.6 us
    all_to_all x1, starting transfers between devices, local(): lax.all_to_all(strain_rate, 'fibre', split_axis=1, concat_axis=0, tiled=T...  5.42 us
    convert_element_type x1, local copies, waits for them, and re-layouts, local(): group_sums.astype(jnp.bfloat16)  4.11 us
  transfers between devices with their start and end apart: 4, of which 4 were waited for; matrix products, arithmetic and copies ran while one was open for 2% of the time, Pallas kernels for 0%

commit v1 on v0

v1 whole, which is shorter than its diff:
```python
import functools
import math

import jax
import jax.numpy as jnp
import numpy as np
from jax import lax
from jax.experimental import pallas as pl
from jax.experimental.pallas import tpu as pltpu
from jax.sharding import PartitionSpec as P
import ml_dtypes

FREQS = 256
OFFS = 64
LAGS = 401
LANES = 128
MESH = pl.DeviceIdType.MESH

water_level = 0.5


def forward_table(seg_length):
    t = np.arange(seg_length)[:, None]
    j = np.arange(1, FREQS + 1)[None, :]
    angles = (2.0 * math.pi / seg_length) * (t * j % seg_length)
    taper = 0.5 - 0.5 * np.cos(2.0 * math.pi / seg_length * t)
    real = (taper * np.cos(angles)).astype(np.float32)
    imag = (-taper * np.sin(angles)).astype(np.float32)
    parts = []
    for h in range(FREQS // LANES):
        cols = slice(h * LANES, (h + 1) * LANES)
        parts += [real[:, cols], imag[:, cols]]
    return np.concatenate(parts, axis=1).astype(ml_dtypes.bfloat16)


def inverse_table(seg_length):
    j = np.arange(1, FREQS + 1)[:, None]
    lag = np.arange(LAGS)[None, :] - (LAGS - 1) // 2
    angles = (2.0 * math.pi / seg_length) * (j * lag % seg_length)
    real, imag = np.cos(angles).astype(np.float32), -np.sin(angles).astype(np.float32)
    parts = []
    for h in range(FREQS // LANES):
        rows = slice(h * LANES, (h + 1) * LANES)
        parts += [real[rows], imag[rows]]
    return np.concatenate(parts, axis=0).astype(ml_dtypes.bfloat16)


def gather_kernel(nf, nt, x_ref, table_ref, g_ref, white, send_sem, recv_sem, pair_send, pair_recv):
    fibre, tm, core = lax.axis_index("fibre"), lax.axis_index("tm"), lax.axis_index("freq")
    segs = nf * nt
    me = fibre * nt + tm
    sibling = {"freq": 1 - core}
    block = x_ref.shape[1] // nf
    rows = block + OFFS

    def device(other):
        return {"fibre": lax.div(other, nt), "tm": lax.rem(other, nt)}

    barrier = pltpu.get_barrier_semaphore()
    pl.semaphore_signal(barrier, inc=1, device_id=sibling, device_id_type=MESH)

    def greet(i, _):
        pl.semaphore_signal(
            barrier, inc=1, device_id=device(lax.rem(me + i, segs)), device_id_type=MESH
        )
        return 0

    lax.fori_loop(1, segs, greet, 0)

    chans = x_ref.shape[1]
    step = 128

    def whiten(i, _):
        here = pl.ds(pl.multiple_of(i * step, step), step)
        spectra = jnp.dot(x_ref[0, here, :], table_ref[...], preferred_element_type=jnp.float32)
        squares = spectra * spectra
        power = jnp.sum(squares, axis=1, keepdims=True) * (1.0 / FREQS)
        floor = (power + 1e-06) * (water_level * water_level)
        for h in range(FREQS // LANES):
            re = slice(2 * h * LANES, (2 * h + 1) * LANES)
            im = slice((2 * h + 1) * LANES, (2 * h + 2) * LANES)
            scale = lax.rsqrt(jnp.maximum(squares[:, re] + squares[:, im], floor))
            white[h, here, 0:LANES] = (spectra[:, re] * scale).astype(jnp.bfloat16)
            white[h, here, LANES : 2 * LANES] = (spectra[:, im] * scale).astype(jnp.bfloat16)
        return 0

    lax.fori_loop(0, chans // step, whiten, 0, unroll=chans <= 512)
    white[:, chans:, :] = jnp.zeros((2, OFFS, 2 * LANES), jnp.bfloat16)

    pl.semaphore_wait(barrier, segs)

    def outgoing(i):
        other = lax.rem(me + i, segs)
        first = pl.multiple_of(lax.div(other, nt) * block, block)
        return pltpu.make_async_remote_copy(
            src_ref=white.at[core, pl.ds(first, rows)],
            dst_ref=g_ref.at[me, core],
            send_sem=send_sem.at[other],
            recv_sem=recv_sem.at[me],
            device_id=device(other),
            device_id_type=MESH,
        )

    def incoming(s):
        return pltpu.make_async_remote_copy(
            src_ref=white.at[core, pl.ds(0, rows)],
            dst_ref=g_ref.at[s, core],
            send_sem=send_sem.at[s],
            recv_sem=recv_sem.at[s],
            device_id=device(s),
            device_id_type=MESH,
        )

    def across(s, half):
        return pltpu.make_async_remote_copy(
            src_ref=g_ref.at[s, half],
            dst_ref=g_ref.at[s, half],
            send_sem=pair_send.at[s],
            recv_sem=pair_recv.at[s],
            device_id=sibling,
            device_id_type=MESH,
        )

    def start(i, _):
        outgoing(i).start()
        return 0

    lax.fori_loop(1, segs, start, 0)

    own = pl.ds(pl.multiple_of(fibre * block, block), rows)
    g_ref[me] = white[:, own, :]

    def forward(i, _):
        s = lax.rem(me + segs - i, segs)
        incoming(s).wait_recv()
        across(s, core).start()
        return 0

    lax.fori_loop(1, segs, forward, 0)

    def finish(i, _):
        s = lax.rem(me + segs - i, segs)
        across(s, 1 - core).wait_recv()
        across(s, core).wait_send()
        outgoing(i).wait_send()
        return 0

    lax.fori_loop(1, segs, finish, 0)


def cross_kernel(segs, group, block, norm, g_ref, inverse_ref, out_ref, right, stacked):
    step = pl.program_id(0)
    halves = FREQS // LANES
    share = group * pl.num_programs(0)
    place = lax.axis_index("tm") * lax.axis_size("freq") + lax.axis_index("freq")
    first = pl.multiple_of(place * share, 8)

    @pl.when(step == 0)
    def _():
        def widen(s, _):
            for h in range(halves):
                for p in range(2):
                    cols = slice(p * LANES, (p + 1) * LANES)
                    right[s, 2 * h + p] = g_ref[s, h, :, cols].astype(jnp.float32)
            return 0

        lax.fori_loop(0, segs, widen, 0)

    base = first + step * group + 1

    def tile(r, _):
        here = pl.ds(pl.multiple_of(r * 8, 8), 8)
        for h in range(halves):
            real = [jnp.zeros((8, LANES), jnp.float32)] * group
            imag = [jnp.zeros((8, LANES), jnp.float32)] * group

            def add(s, real, imag):
                a0, a1 = right[s, 2 * h, here, :], right[s, 2 * h + 1, here, :]
                for k in range(group):
                    there = pl.ds(base + (r * 8 + k), 8)
                    b0, b1 = right[s, 2 * h, there, :], right[s, 2 * h + 1, there, :]
                    real[k] = real[k] + (a0 * b0 + a1 * b1)
                    imag[k] = imag[k] + (a1 * b0 - a0 * b1)

            if segs <= 16:
                for s in range(segs):
                    add(s, real, imag)
            else:

                def body(s, carry):
                    real, imag = list(carry[0]), list(carry[1])
                    add(s, real, imag)
                    return tuple(real), tuple(imag)

                real, imag = lax.fori_loop(0, segs, body, (tuple(real), tuple(imag)))
            for k in range(group):
                at = pl.ds(pl.multiple_of(k * block + r * 8, 8), 8)
                stacked[at, 2 * h * LANES : (2 * h + 1) * LANES] = real[k]
                stacked[at, (2 * h + 1) * LANES : (2 * h + 2) * LANES] = imag[k]
        return 0

    lax.fori_loop(0, block // 8, tile, 0)
    terms = jnp.dot(
        stacked[...].astype(jnp.bfloat16), inverse_ref[...], preferred_element_type=jnp.float32
    )
    out_ref[...] = (terms * norm).reshape(group, block, LAGS)


def local(nf, nt, nq, strain_rate):
    _, chans, seg_length = strain_rate.shape
    segs = nf * nt
    block = chans // nf
    rows = block + OFFS
    share = OFFS // (nt * nq)
    group = 4
    vmem = pl.BlockSpec(memory_space=pltpu.VMEM)
    gathered = pl.pallas_call(
        functools.partial(gather_kernel, nf, nt),
        out_shape=jax.ShapeDtypeStruct((segs, 2, rows, 2 * LANES), jnp.bfloat16),
        in_specs=[vmem, vmem],
        out_specs=vmem,
        scratch_shapes=[
            pltpu.VMEM((2, chans + OFFS, 2 * LANES), jnp.bfloat16),
            pltpu.SemaphoreType.DMA((segs,)),
            pltpu.SemaphoreType.DMA((segs,)),
            pltpu.SemaphoreType.DMA((segs,)),
            pltpu.SemaphoreType.DMA((segs,)),
        ],
        compiler_params=pltpu.CompilerParams(
            collective_id=0, has_side_effects=True, vmem_limit_bytes=48 << 20
        ),
    )(strain_rate, jnp.asarray(forward_table(seg_length)))
    norm = 1.0 / math.sqrt(segs * FREQS)
    return pl.pallas_call(
        functools.partial(cross_kernel, segs, group, block, norm),
        grid=(share // group,),
        out_shape=jax.ShapeDtypeStruct((share, block, LAGS), jnp.float32),
        in_specs=[vmem, vmem],
        out_specs=pl.BlockSpec((group, block, LAGS), lambda i: (i, 0, 0)),
        scratch_shapes=[
            pltpu.VMEM((segs, 4, rows, LANES), jnp.float32),
            pltpu.VMEM((group * block, 2 * FREQS), jnp.float32),
        ],
        compiler_params=pltpu.CompilerParams(
            dimension_semantics=("arbitrary",),
            vmem_limit_bytes=(32 << 20) if segs <= 32 else (60 << 20),
        ),
    )(gathered, jnp.asarray(inverse_table(seg_length)))


def solution(mesh):
    sizes = mesh.shape
    return jax.shard_map(
        functools.partial(local, sizes["fibre"], sizes["tm"], sizes["freq"]),
        mesh=mesh,
        in_specs=(P(("fibre", "tm"), "groups", None),),
        out_specs=P(("tm", "freq"), ("groups", "fibre"), None),
        check_vma=False,
    )
```

time: 163 us -> 25.5 us (0.16)
  the two profiles are of different devices: /device:TPU:1 before, /device:TPU:11 now
where the time goes in v1:
time: 25.5 us; the launch traced here: 25.3 us
  Pallas kernels  23.1 us (91%)
  local copies, waits for them, and re-layouts  2.27 us (9%)
    pallas_call x1, Pallas kernels, local(): pl.pallas_call(functools.partial(gather_kernel, nf, nt), out_shape=jax.Sh...  17.4 us
    pallas_call x1, Pallas kernels, local(): pl.pallas_call(functools.partial(cross_kernel, segs, group, block, norm),...  5.63 us
    unnamed x6, local copies, waits for them, and re-layouts  2.27 us

profile of v1, /device:TPU:11, one launch (start us, length us, event | category | flops | bytes accessed | tf_op | source)
XLA Modules:
  0.0 25.3 jit_solution(9640647817138613962)
XLA Ops:
  0.0 0.0 copy-start
  0.0 1.2 %copy-done = bf16[1024,512]{1,0:T(8,128)(2,1)S(1)} copy-done((bf16[1024,512]{1,0:T(8,128)(2,1)S(1)}, bf16[1024,512]{1,0:T(8,128)(2,1)}, u32[]{:S(2)}) %copy-start) | copy-done | bytes 1048600
  1.2 0.0 copy-start.1
  1.2 1.0 %copy-done.1 = bf16[1,256,1024]{2,1,0:T(8,128)(2,1)S(1)} copy-done((bf16[1,256,1024]{2,1,0:T(8,128)(2,1)S(1)}, bf16[1,256,1024]{2,1,0:T(8,128)(2,1)}, u32[]{:S(2)}) %copy-start.1) | copy-done | bytes 524312
  2.3 0.0 copy-start.2
  2.3 17.4 %shard_map.37.g_ref = bf16[8,2,128,256]{3,2,1,0:T(8,128)(2,1)S(1)} custom-call(bf16[1,256,1024]{2,1,0:T(8,128)(2,1)S(1)} %copy-done.1, bf16[1024,512]{1,0:T(8,128)(2,1)S(1)} %copy-done), custom_call_target="tpu_custom_call" | custom-call | tf_op jit(solution)/shard_map/pallas_call | solution.py:217
  19.7 0.0 copy-done.2
  19.7 5.6 %shard_map.38 = f32[16,64,401]{2,1,0:T(8,128)} custom-call(bf16[8,2,128,256]{3,2,1,0:T(8,128)(2,1)S(1)} %shard_map.37.g_ref, bf16[512,401]{1,0:T(8,128)(2,1)S(1)} %copy-done.2), custom_call_target="tpu_custom_call" | custom-call | tf_op jit(solution)/shard_map/pallas_call | solution.py:234
Async XLA Ops:
  0.0 1.2 %copy-start = (bf16[1024,512]{1,0:T(8,128)(2,1)S(1)}, bf16[1024,512]{1,0:T(8,128)(2,1)}, u32[]{:S(2)}) copy-start(bf16[1024,512]{1,0:T(8,128)(2,1)} %constant.4.clone.table_ref) | copy-start | bytes 3145732
  1.2 1.0 %copy-start.1 = (bf16[1,256,1024]{2,1,0:T(8,128)(2,1)S(1)}, bf16[1,256,1024]{2,1,0:T(8,128)(2,1)}, u32[]{:S(2)}) copy-start(bf16[1,256,1024]{2,1,0:T(8,128)(2,1)} %x_ref.1) | copy-start | bytes 1572868
  2.3 17.4 %copy-start.2 = (bf16[512,401]{1,0:T(8,128)(2,1)S(1)}, bf16[512,401]{1,0:T(8,128)(2,1)}, u32[]{:S(2)}) copy-start(bf16[512,401]{1,0:T(8,128)(2,1)} %constant.5.clone.inverse_ref) | copy-start | bytes 1231876

commit v2 on v1

--- a/solution.py
+++ b/solution.py
@@ -45,34 +45,49 @@
     return np.concatenate(parts, axis=0).astype(ml_dtypes.bfloat16)
 
 
-def gather_kernel(nf, nt, x_ref, table_ref, g_ref, white, send_sem, recv_sem, pair_send, pair_recv):
+def gather_kernel(
+    nf, nt, x_hbm, table_hbm, g_ref, x_ref, table_ref, white,
+    load_sem, fibre_send, tm_send, recv_sem, pair_send, pair_recv,
+):
     fibre, tm, core = lax.axis_index("fibre"), lax.axis_index("tm"), lax.axis_index("freq")
-    segs = nf * nt
     me = fibre * nt + tm
     sibling = {"freq": 1 - core}
-    block = x_ref.shape[1] // nf
+    chans = x_ref.shape[0]
+    block = chans // nf
     rows = block + OFFS
-
-    def device(other):
-        return {"fibre": lax.div(other, nt), "tm": lax.rem(other, nt)}
+    step = 128
+    steps = chans // step
+    depth = table_ref.shape[0] // 4
+
+    def load_x(i):
+        here = pl.ds(pl.multiple_of(i * step, step), step)
+        return pltpu.make_async_copy(x_hbm.at[0, here], x_ref.at[here], load_sem.at[4 + i])
+
+    def load_table(i):
+        here = pl.ds(i * depth, depth)
+        return pltpu.make_async_copy(table_hbm.at[here], table_ref.at[here], load_sem.at[i])
+
+    for i in range(4):
+        load_table(i).start()
+    for i in range(steps):
+        load_x(i).start()
 
     barrier = pltpu.get_barrier_semaphore()
     pl.semaphore_signal(barrier, inc=1, device_id=sibling, device_id_type=MESH)
-
-    def greet(i, _):
-        pl.semaphore_signal(
-            barrier, inc=1, device_id=device(lax.rem(me + i, segs)), device_id_type=MESH
-        )
-        return 0
-
-    lax.fori_loop(1, segs, greet, 0)
-
-    chans = x_ref.shape[1]
-    step = 128
+    for i in range(1, nf):
+        to = {"fibre": lax.rem(fibre + i, nf)}
+        pl.semaphore_signal(barrier, inc=1, device_id=to, device_id_type=MESH)
+    for i in range(1, nt):
+        to = {"tm": lax.rem(tm + i, nt)}
+        pl.semaphore_signal(barrier, inc=1, device_id=to, device_id_type=MESH)
+
+    for i in range(4):
+        load_table(i).wait()
 
     def whiten(i, _):
         here = pl.ds(pl.multiple_of(i * step, step), step)
-        spectra = jnp.dot(x_ref[0, here, :], table_ref[...], preferred_element_type=jnp.float32)
+        load_x(i).wait()
+        spectra = jnp.dot(x_ref[here, :], table_ref[...], preferred_element_type=jnp.float32)
         squares = spectra * spectra
         power = jnp.sum(squares, axis=1, keepdims=True) * (1.0 / FREQS)
         floor = (power + 1e-06) * (water_level * water_level)
@@ -84,30 +99,44 @@
             white[h, here, LANES : 2 * LANES] = (spectra[:, im] * scale).astype(jnp.bfloat16)
         return 0
 
-    lax.fori_loop(0, chans // step, whiten, 0, unroll=chans <= 512)
     white[:, chans:, :] = jnp.zeros((2, OFFS, 2 * LANES), jnp.bfloat16)
-
-    pl.semaphore_wait(barrier, segs)
-
-    def outgoing(i):
-        other = lax.rem(me + i, segs)
-        first = pl.multiple_of(lax.div(other, nt) * block, block)
+    lax.fori_loop(0, steps, whiten, 0, unroll=steps <= 4)
+
+    pl.semaphore_wait(barrier, nf + nt - 1)
+
+    def own_rows(f):
+        return pl.ds(pl.multiple_of(f * block, block), rows)
+
+    def along_fibre(i):
+        f = lax.rem(fibre + i, nf)
         return pltpu.make_async_remote_copy(
-            src_ref=white.at[core, pl.ds(first, rows)],
+            src_ref=white.at[core, own_rows(f)],
             dst_ref=g_ref.at[me, core],
-            send_sem=send_sem.at[other],
+            send_sem=fibre_send.at[i],
             recv_sem=recv_sem.at[me],
-            device_id=device(other),
+            device_id={"fibre": f},
             device_id_type=MESH,
         )
 
-    def incoming(s):
+    def along_tm(j, i):
+        s = lax.rem(fibre + nf - j, nf) * nt + tm
+        own = isinstance(j, int) and j == 0
         return pltpu.make_async_remote_copy(
-            src_ref=white.at[core, pl.ds(0, rows)],
+            src_ref=white.at[core, own_rows(fibre)] if own else g_ref.at[s, core],
             dst_ref=g_ref.at[s, core],
-            send_sem=send_sem.at[s],
+            send_sem=tm_send.at[j, i],
             recv_sem=recv_sem.at[s],
-            device_id=device(s),
+            device_id={"tm": lax.rem(tm + i, nt)},
+            device_id_type=MESH,
+        )
+
+    def arrived(s):
+        return pltpu.make_async_remote_copy(
+            src_ref=g_ref.at[s, core],
+            dst_ref=g_ref.at[s, core],
+            send_sem=pair_send.at[s],
+            recv_sem=recv_sem.at[s],
+            device_id=sibling,
             device_id_type=MESH,
         )
 
@@ -121,31 +150,48 @@
             device_id_type=MESH,
         )
 
-    def start(i, _):
-        outgoing(i).start()
-        return 0
-
-    lax.fori_loop(1, segs, start, 0)
-
-    own = pl.ds(pl.multiple_of(fibre * block, block), rows)
-    g_ref[me] = white[:, own, :]
-
-    def forward(i, _):
-        s = lax.rem(me + segs - i, segs)
-        incoming(s).wait_recv()
+    def loop(low, high, body):
+        if high - low <= 8:
+            for i in range(low, high):
+                body(i)
+        else:
+            lax.fori_loop(low, high, lambda i, _: (body(i), 0)[1], 0)
+
+    for i in range(1, nt):
+        along_tm(0, i).start()
+    loop(1, nf, lambda i: along_fibre(i).start())
+    g_ref[me] = white[:, own_rows(fibre), :]
+
+    def column(j):
+        s = lax.rem(fibre + nf - j, nf) * nt + tm
+        arrived(s).wait_recv()
+        for i in range(1, nt):
+            along_tm(j, i).start()
         across(s, core).start()
-        return 0
-
-    lax.fori_loop(1, segs, forward, 0)
-
-    def finish(i, _):
-        s = lax.rem(me + segs - i, segs)
-        across(s, 1 - core).wait_recv()
-        across(s, core).wait_send()
-        outgoing(i).wait_send()
-        return 0
-
-    lax.fori_loop(1, segs, finish, 0)
+
+    loop(1, nf, column)
+
+    def others(j):
+        for i in range(1, nt):
+            s = lax.rem(fibre + nf - j, nf) * nt + lax.rem(tm + nt - i, nt)
+            arrived(s).wait_recv()
+            across(s, core).start()
+
+    loop(0, nf, others)
+
+    def finish(j):
+        for i in range(nt):
+            s = lax.rem(fibre + nf - j, nf) * nt + lax.rem(tm + nt - i, nt)
+            if i > 0 or not (isinstance(j, int) and j == 0):
+                across(s, 1 - core).wait_recv()
+                across(s, core).wait_send()
+        for i in range(1, nt):
+            along_tm(j, i).wait_send()
+        if not (isinstance(j, int) and j == 0):
+            along_fibre(j).wait_send()
+
+    finish(0)
+    loop(1, nf, finish)
 
 
 def cross_kernel(segs, group, block, norm, g_ref, inverse_ref, out_ref, right, stacked):
@@ -217,11 +263,15 @@
     gathered = pl.pallas_call(
         functools.partial(gather_kernel, nf, nt),
         out_shape=jax.ShapeDtypeStruct((segs, 2, rows, 2 * LANES), jnp.bfloat16),
-        in_specs=[vmem, vmem],
+        in_specs=[pl.BlockSpec(memory_space=pl.ANY)] * 2,
         out_specs=vmem,
         scratch_shapes=[
+            pltpu.VMEM((chans, seg_length), jnp.bfloat16),
+            pltpu.VMEM((seg_length, 2 * FREQS), jnp.bfloat16),
             pltpu.VMEM((2, chans + OFFS, 2 * LANES), jnp.bfloat16),
-            pltpu.SemaphoreType.DMA((segs,)),
+            pltpu.SemaphoreType.DMA((4 + chans // 128,)),
+            pltpu.SemaphoreType.DMA((nf,)),
+            pltpu.SemaphoreType.DMA((nf, nt)),
             pltpu.SemaphoreType.DMA((segs,)),
             pltpu.SemaphoreType.DMA((segs,)),
             pltpu.SemaphoreType.DMA((segs,)),

time: 25.5 us -> 24.9 us (0.976)
  the two profiles are of different devices: /device:TPU:11 before, /device:TPU:1 now
where the time goes in v2:
time: 24.9 us; the launch traced here: 24.6 us
  Pallas kernels  22.3 us (90%)
  local copies, waits for them, and re-layouts  2.27 us (9%)
    pallas_call x1, Pallas kernels, local(): pl.pallas_call(functools.partial(gather_kernel, nf, nt), out_shape=jax.Sh...  16.7 us
    pallas_call x1, Pallas kernels, local(): pl.pallas_call(functools.partial(cross_kernel, segs, group, block, norm),...  5.6 us
    unnamed x6, local copies, waits for them, and re-layouts  2.27 us

profile of v2, /device:TPU:1, one launch (start us, length us, event | category | flops | bytes accessed | tf_op | source)
XLA Modules:
  0.0 24.6 jit_solution(14289243552248149025)
XLA Ops:
  0.0 0.0 copy-start
  0.0 1.2 %copy-done = bf16[1024,512]{1,0:T(8,128)(2,1)S(1)} copy-done((bf16[1024,512]{1,0:T(8,128)(2,1)S(1)}, bf16[1024,512]{1,0:T(8,128)(2,1)}, u32[]{:S(2)}) %copy-start) | copy-done | bytes 1048600
  1.2 0.0 copy-start.1
  1.2 1.0 %copy-done.1 = bf16[1,256,1024]{2,1,0:T(8,128)(2,1)S(1)} copy-done((bf16[1,256,1024]{2,1,0:T(8,128)(2,1)S(1)}, bf16[1,256,1024]{2,1,0:T(8,128)(2,1)}, u32[]{:S(2)}) %copy-start.1) | copy-done | bytes 524312
  2.3 0.0 copy-start.2
  2.3 16.7 %shard_map.37.g_ref = bf16[8,2,128,256]{3,2,1,0:T(8,128)(2,1)S(1)} custom-call(bf16[1,256,1024]{2,1,0:T(8,128)(2,1)S(1)} %copy-done.1, bf16[1024,512]{1,0:T(8,128)(2,1)S(1)} %copy-done), custom_call_target="tpu_custom_call" | custom-call | tf_op jit(solution)/shard_map/pallas_call | solution.py:263
  19.0 0.0 copy-done.2
  19.0 5.6 %shard_map.38 = f32[16,64,401]{2,1,0:T(8,128)} custom-call(bf16[8,2,128,256]{3,2,1,0:T(8,128)(2,1)S(1)} %shard_map.37.g_ref, bf16[512,401]{1,0:T(8,128)(2,1)S(1)} %copy-done.2), custom_call_target="tpu_custom_call" | custom-call | tf_op jit(solution)/shard_map/pallas_call | solution.py:284
Async XLA Ops:
  0.0 1.2 %copy-start = (bf16[1024,512]{1,0:T(8,128)(2,1)S(1)}, bf16[1024,512]{1,0:T(8,128)(2,1)}, u32[]{:S(2)}) copy-start(bf16[1024,512]{1,0:T(8,128)(2,1)} %constant.4.clone.table_hbm) | copy-start | bytes 3145732
  1.2 1.0 %copy-start.1 = (bf16[1,256,1024]{2,1,0:T(8,128)(2,1)S(1)}, bf16[1,256,1024]{2,1,0:T(8,128)(2,1)}, u32[]{:S(2)}) copy-start(bf16[1,256,1024]{2,1,0:T(8,128)(2,1)} %x_hbm.1) | copy-start | bytes 1572868
  2.3 16.7 %copy-start.2 = (bf16[512,401]{1,0:T(8,128)(2,1)S(1)}, bf16[512,401]{1,0:T(8,128)(2,1)}, u32[]{:S(2)}) copy-start(bf16[512,401]{1,0:T(8,128)(2,1)} %constant.5.clone.inverse_ref) | copy-start | bytes 1231876

commit v3 on v2

v3 whole, which is shorter than its diff:
```python
import functools
import math

import jax
import jax.numpy as jnp
import numpy as np
from jax import lax
from jax.experimental import pallas as pl
from jax.experimental.pallas import tpu as pltpu
from jax.sharding import PartitionSpec as P
import ml_dtypes

FREQS = 256
OFFS = 64
LAGS = 401
LANES = 128
MESH = pl.DeviceIdType.MESH

water_level = 0.5


def forward_table(seg_length):
    t = np.arange(seg_length)[:, None]
    j = np.arange(1, FREQS + 1)[None, :]
    angles = (2.0 * math.pi / seg_length) * (t * j % seg_length)
    taper = 0.5 - 0.5 * np.cos(2.0 * math.pi / seg_length * t)
    real = (taper * np.cos(angles)).astype(np.float32)
    imag = (-taper * np.sin(angles)).astype(np.float32)
    parts = []
    for h in range(FREQS // LANES):
        cols = slice(h * LANES, (h + 1) * LANES)
        parts += [real[:, cols], imag[:, cols]]
    return np.concatenate(parts, axis=1).astype(ml_dtypes.bfloat16)


def inverse_table(seg_length):
    j = np.arange(1, FREQS + 1)[:, None]
    lag = np.arange(LAGS)[None, :] - (LAGS - 1) // 2
    angles = (2.0 * math.pi / seg_length) * (j * lag % seg_length)
    real, imag = np.cos(angles).astype(np.float32), -np.sin(angles).astype(np.float32)
    parts = []
    for h in range(FREQS // LANES):
        rows = slice(h * LANES, (h + 1) * LANES)
        parts += [real[rows], imag[rows]]
    return np.concatenate(parts, axis=0).astype(ml_dtypes.bfloat16)


def accumulate(load, spectra, acc, count, first, share, block, fresh):
    halves = FREQS // LANES
    for n in range(count):
        for h in range(halves):
            wide = load(n, h).astype(jnp.float32)
            spectra[n, 2 * h] = wide[:, :LANES]
            spectra[n, 2 * h + 1] = wide[:, LANES:]

    def tile(r, _):
        here = pl.ds(pl.multiple_of(r * 8, 8), 8)
        for h in range(halves):
            re = slice(2 * h * LANES, (2 * h + 1) * LANES)
            im = slice((2 * h + 1) * LANES, (2 * h + 2) * LANES)
            a0 = [spectra[n, 2 * h, here, :] for n in range(count)]
            a1 = [spectra[n, 2 * h + 1, here, :] for n in range(count)]
            for k in range(share):
                at = pl.ds(pl.multiple_of(k * block + r * 8, 8), 8)
                there = pl.ds(first + (r * 8 + k + 1), 8)
                real = imag = None
                for n in range(count):
                    b0, b1 = spectra[n, 2 * h, there, :], spectra[n, 2 * h + 1, there, :]
                    x, y = a0[n] * b0 + a1[n] * b1, a1[n] * b0 - a0[n] * b1
                    real = x if real is None else real + x
                    imag = y if imag is None else imag + y
                acc[at, re] = real if fresh else acc[at, re] + real
                acc[at, im] = imag if fresh else acc[at, im] + imag
        return 0

    lax.fori_loop(0, block // 8, tile, 0)


def stack_kernel(
    nf, nt, nq, x_hbm, table_hbm, acc, x_ref, table_ref, white, g_ref, spectra_ref,
    load_sem, fibre_send, tm_send, recv_sem, pair_send, pair_recv,
):
    fibre, tm, core = lax.axis_index("fibre"), lax.axis_index("tm"), lax.axis_index("freq")
    me = fibre * nt + tm
    sibling = {"freq": 1 - core}
    chans = x_ref.shape[0]
    block = chans // nf
    rows = block + OFFS
    chunks = 2
    part = rows // chunks
    step = 128
    steps = chans // step
    depth = table_ref.shape[0] // 4

    def load_x(i):
        here = pl.ds(pl.multiple_of(i * step, step), step)
        return pltpu.make_async_copy(x_hbm.at[0, here], x_ref.at[here], load_sem.at[4 + i])

    def load_table(i):
        here = pl.ds(i * depth, depth)
        return pltpu.make_async_copy(table_hbm.at[here], table_ref.at[here], load_sem.at[i])

    for i in range(4):
        load_table(i).start()
    for i in range(steps):
        load_x(i).start()

    barrier = pltpu.get_barrier_semaphore()
    pl.semaphore_signal(barrier, inc=1, device_id=sibling, device_id_type=MESH)
    for i in range(1, nf):
        to = {"fibre": lax.rem(fibre + i, nf)}
        pl.semaphore_signal(barrier, inc=1, device_id=to, device_id_type=MESH)
    for i in range(1, nt):
        to = {"tm": lax.rem(tm + i, nt)}
        pl.semaphore_signal(barrier, inc=1, device_id=to, device_id_type=MESH)

    for i in range(4):
        load_table(i).wait()

    def whiten(i, _):
        here = pl.ds(pl.multiple_of(i * step, step), step)
        load_x(i).wait()
        spectra = jnp.dot(x_ref[here, :], table_ref[...], preferred_element_type=jnp.float32)
        squares = spectra * spectra
        power = jnp.sum(squares, axis=1, keepdims=True) * (1.0 / FREQS)
        floor = (power + 1e-06) * (water_level * water_level)
        for h in range(FREQS // LANES):
            re = slice(2 * h * LANES, (2 * h + 1) * LANES)
            im = slice((2 * h + 1) * LANES, (2 * h + 2) * LANES)
            scale = lax.rsqrt(jnp.maximum(squares[:, re] + squares[:, im], floor))
            white[h, here, 0:LANES] = (spectra[:, re] * scale).astype(jnp.bfloat16)
            white[h, here, LANES : 2 * LANES] = (spectra[:, im] * scale).astype(jnp.bfloat16)
        return 0

    white[:, chans:, :] = jnp.zeros((2, OFFS, 2 * LANES), jnp.bfloat16)
    lax.fori_loop(0, steps, whiten, 0, unroll=steps <= 4)

    pl.semaphore_wait(barrier, nf + nt - 1)

    def rows_of(f, c):
        return pl.ds(pl.multiple_of(f * block + c * part, 16), part)

    def landing(s, c):
        return g_ref.at[s, core, pl.ds(c * part, part)]

    def along_fibre(f, c):
        return pltpu.make_async_remote_copy(
            src_ref=white.at[core, rows_of(f, c)],
            dst_ref=landing(me, c),
            send_sem=fibre_send.at[f, c],
            recv_sem=recv_sem.at[me, c],
            device_id={"fibre": f},
            device_id_type=MESH,
        )

    def along_tm(f, i, c, own=False):
        s = f * nt + tm
        return pltpu.make_async_remote_copy(
            src_ref=white.at[core, rows_of(fibre, c)] if own else landing(s, c),
            dst_ref=landing(s, c),
            send_sem=tm_send.at[f, i, c],
            recv_sem=recv_sem.at[s, c],
            device_id={"tm": lax.rem(tm + i, nt)},
            device_id_type=MESH,
        )

    def arrived(s, c):
        return pltpu.make_async_remote_copy(
            src_ref=landing(s, c),
            dst_ref=landing(s, c),
            send_sem=pair_send.at[s],
            recv_sem=recv_sem.at[s, c],
            device_id=sibling,
            device_id_type=MESH,
        )

    def across(s, half):
        return pltpu.make_async_remote_copy(
            src_ref=g_ref.at[s, half],
            dst_ref=g_ref.at[s, half],
            send_sem=pair_send.at[s],
            recv_sem=pair_recv.at[s],
            device_id=sibling,
            device_id_type=MESH,
        )

    def loop(low, high, body):
        if high - low <= 8:
            for i in range(low, high):
                body(i)
        else:
            lax.fori_loop(low, high, lambda i, _: (body(i), 0)[1], 0)

    def nearest_first(body):
        def at_distance(d):
            for f in (fibre + d, fibre - d):
                pl.when(jnp.logical_and(f >= 0, f < nf))(functools.partial(body, f))

        loop(1, nf, at_distance)

    for c in range(chunks):
        for i in range(1, nt):
            along_tm(fibre, i, c, own=True).start()

    @nearest_first
    def _(f):
        for c in range(chunks):
            along_fibre(f, c).start()

    g_ref[me] = jnp.stack(
        [white[h, pl.ds(pl.multiple_of(fibre * block, 16), rows), :] for h in range(2)]
    )

    @nearest_first
    def _(f):
        s = f * nt + tm
        for c in range(chunks):
            arrived(s, c).wait_recv()
            for i in range(1, nt):
                along_tm(f, i, c).start()
        across(s, core).start()

    share = acc.shape[0] // block
    place = tm * nq + core
    first = place * share

    @nearest_first
    def _(f):
        across(f * nt + tm, 1 - core).wait_recv()

    def add(batch, index, fresh):
        def load(n, h):
            return g_ref[index(n), h]

        accumulate(load, spectra_ref, acc, batch, first, share, block, fresh)

    batch = math.gcd(nf, 4)
    add(batch, lambda n: n * nt + tm, True)
    if nf > batch:
        loop(1, nf // batch, lambda i: add(batch, lambda n: (i * batch + n) * nt + tm, False))

    def pass_on(f):
        for i in range(1, nt):
            s = f * nt + lax.rem(tm + i, nt)
            for c in range(chunks):
                arrived(s, c).wait_recv()
            across(s, core).start()

    pass_on(fibre)
    nearest_first(pass_on)
    for i in range(1, nt):
        other = lax.rem(tm + i, nt)

        def part_of(b):
            for n in range(batch):
                across((b * batch + n) * nt + other, 1 - core).wait_recv()
            add(batch, lambda n: (b * batch + n) * nt + other, False)

        loop(0, nf // batch, part_of)

    for i in range(1, nt):
        across(fibre * nt + lax.rem(tm + i, nt), core).wait_send()
        for c in range(chunks):
            along_tm(fibre, i, c, own=True).wait_send()

    @nearest_first
    def _(f):
        for c in range(chunks):
            along_fibre(f, c).wait_send()
        for i in range(nt):
            across(f * nt + lax.rem(tm + i, nt), core).wait_send()
            if i > 0:
                for c in range(chunks):
                    along_tm(f, i, c).wait_send()


def lag_kernel(norm, stacked_ref, inverse_ref, out_ref):
    terms = jnp.dot(
        stacked_ref[...].astype(jnp.bfloat16), inverse_ref[...], preferred_element_type=jnp.float32
    )
    out_ref[...] = (terms * norm).reshape(out_ref.shape)


def local(nf, nt, nq, strain_rate):
    _, chans, seg_length = strain_rate.shape
    segs = nf * nt
    block = chans // nf
    rows = block + OFFS
    share = OFFS // (nt * nq)
    group = 4
    vmem = pl.BlockSpec(memory_space=pltpu.VMEM)
    stacked = pl.pallas_call(
        functools.partial(stack_kernel, nf, nt, nq),
        out_shape=jax.ShapeDtypeStruct((share * block, 2 * FREQS), jnp.float32),
        in_specs=[pl.BlockSpec(memory_space=pltpu.HBM)] * 2,
        out_specs=vmem,
        scratch_shapes=[
            pltpu.VMEM((chans, seg_length), jnp.bfloat16),
            pltpu.VMEM((seg_length, 2 * FREQS), jnp.bfloat16),
            pltpu.VMEM((2, chans + OFFS, 2 * LANES), jnp.bfloat16),
            pltpu.VMEM((segs, 2, rows, 2 * LANES), jnp.bfloat16),
            pltpu.VMEM((math.gcd(nf, 4), 4, rows, LANES), jnp.float32),
            pltpu.SemaphoreType.DMA((4 + chans // 128,)),
            pltpu.SemaphoreType.DMA((nf, 2)),
            pltpu.SemaphoreType.DMA((nf, nt, 2)),
            pltpu.SemaphoreType.DMA((segs, 2)),
            pltpu.SemaphoreType.DMA((segs,)),
            pltpu.SemaphoreType.DMA((segs,)),
        ],
        compiler_params=pltpu.CompilerParams(
            collective_id=0, has_side_effects=True, vmem_limit_bytes=60 << 20
        ),
    )(strain_rate, jnp.asarray(forward_table(seg_length)))
    norm = 1.0 / math.sqrt(segs * FREQS)
    return pl.pallas_call(
        functools.partial(lag_kernel, norm),
        grid=(share // group,),
        out_shape=jax.ShapeDtypeStruct((share, block, LAGS), jnp.float32),
        in_specs=[
            pl.BlockSpec((group * block, 2 * FREQS), lambda i: (i, 0)),
            pl.BlockSpec((2 * FREQS, LAGS), lambda i: (0, 0)),
        ],
        out_specs=pl.BlockSpec((group, block, LAGS), lambda i: (i, 0, 0)),
        compiler_params=pltpu.CompilerParams(dimension_semantics=("arbitrary",)),
    )(stacked, jnp.asarray(inverse_table(seg_length)))


def solution(mesh):
    sizes = mesh.shape
    return jax.shard_map(
        functools.partial(local, sizes["fibre"], sizes["tm"], sizes["freq"]),
        mesh=mesh,
        in_specs=(P(("fibre", "tm"), "groups", None),),
        out_specs=P(("tm", "freq"), ("groups", "fibre"), None),
        check_vma=False,
    )
```

time: 24.9 us -> 25.5 us (1.024)
  Pallas kernels: 22.3 us -> 25.3 us
  local copies, waits for them, and re-layouts: 2.27 us -> 0 us
    pallas_call x2, Pallas kernels: 22.3 us -> 25.3 us  [the longest x1 20.8 us: local(): pl.pallas_call(functools.partial(stack_kernel, nf, nt, nq), out_shape=jax...]
    unnamed x6 -> x0, local copies, waits for them, and re-layouts: 2.27 us -> none
where the time goes in v3:
time: 25.5 us; the launch traced here: 25.3 us
  Pallas kernels  25.3 us (99%)
    pallas_call x1, Pallas kernels, local(): pl.pallas_call(functools.partial(stack_kernel, nf, nt, nq), out_shape=jax...  20.8 us
    pallas_call x1, Pallas kernels, local(): pl.pallas_call(functools.partial(lag_kernel, norm), grid=(share // group,...  4.49 us

profile of v3, /device:TPU:1, one launch (start us, length us, event | category | flops | bytes accessed | tf_op | source)
XLA Modules:
  0.0 25.3 jit_solution(14572436914528183461)
XLA Ops:
  0.0 20.8 %shard_map.37.stacked_ref = f32[1024,512]{1,0:T(8,128)} custom-call(bf16[1,256,1024]{2,1,0:T(8,128)(2,1)} %x_hbm.1, bf16[1024,512]{1,0:T(8,128)(2,1)} %constant.4.clone.table_hbm), custom_call_target="tpu_custom_call" | custom-call | tf_op jit(solution)/shard_map/pallas_call | solution.py:292
  20.8 4.5 %shard_map.38 = f32[16,64,401]{2,1,0:T(8,128)} custom-call(f32[1024,512]{1,0:T(8,128)} %shard_map.37.stacked_ref, bf16[512,401]{1,0:T(8,128)(2,1)} %constant.5.clone.inverse_ref), custom_call_target="tpu_custom_call" | custom-call | tf_op jit(solution)/shard_map/pallas_call | solution.py:315

commit v4 on v3

--- a/solution.py
+++ b/solution.py
@@ -43,6 +43,17 @@
         rows = slice(h * LANES, (h + 1) * LANES)
         parts += [real[rows], imag[rows]]
     return np.concatenate(parts, axis=0).astype(ml_dtypes.bfloat16)
+
+
+TABLE_ROWS = 6144
+
+
+def tables(seg_length):
+    forward, inverse = forward_table(seg_length), inverse_table(seg_length)
+    both = np.zeros((max(TABLE_ROWS, seg_length + 2 * FREQS), 2 * FREQS), ml_dtypes.bfloat16)
+    both[:seg_length] = forward
+    both[seg_length : seg_length + 2 * FREQS, :LAGS] = inverse
+    return both
 
 
 def accumulate(load, spectra, acc, count, first, share, block, fresh):
@@ -77,7 +88,8 @@
 
 
 def stack_kernel(
-    nf, nt, nq, x_hbm, table_hbm, acc, x_ref, table_ref, white, g_ref, spectra_ref,
+    nf, nt, nq, norm, x_hbm, table_hbm, out_ref,
+    acc, x_ref, table_ref, inverse_ref, white, g_ref, spectra_ref,
     load_sem, fibre_send, tm_send, recv_sem, pair_send, pair_recv,
 ):
     fibre, tm, core = lax.axis_index("fibre"), lax.axis_index("tm"), lax.axis_index("freq")
@@ -94,7 +106,7 @@
 
     def load_x(i):
         here = pl.ds(pl.multiple_of(i * step, step), step)
-        return pltpu.make_async_copy(x_hbm.at[0, here], x_ref.at[here], load_sem.at[4 + i])
+        return pltpu.make_async_copy(x_hbm.at[0, here], x_ref.at[here], load_sem.at[5 + i])
 
     def load_table(i):
         here = pl.ds(i * depth, depth)
@@ -104,6 +116,10 @@
         load_table(i).start()
     for i in range(steps):
         load_x(i).start()
+    load_inverse = pltpu.make_async_copy(
+        table_hbm.at[pl.ds(table_ref.shape[0], 2 * FREQS)], inverse_ref, load_sem.at[4]
+    )
+    load_inverse.start()
 
     barrier = pltpu.get_barrier_semaphore()
     pl.semaphore_signal(barrier, inc=1, device_id=sibling, device_id_type=MESH)
@@ -258,6 +274,15 @@
 
         loop(0, nf // batch, part_of)
 
+    load_inverse.wait()
+    group = 4
+    for k in range(share // group):
+        here = slice(k * group * block, (k + 1) * group * block)
+        terms = jnp.dot(
+            acc[here, :].astype(jnp.bfloat16), inverse_ref[...], preferred_element_type=jnp.float32
+        )
+        out_ref[k * group : (k + 1) * group] = (terms[:, :LAGS] * norm).reshape(group, block, LAGS)
+
     for i in range(1, nt):
         across(fibre * nt + lax.rem(tm + i, nt), core).wait_send()
         for c in range(chunks):
@@ -274,33 +299,28 @@
                     along_tm(f, i, c).wait_send()
 
 
-def lag_kernel(norm, stacked_ref, inverse_ref, out_ref):
-    terms = jnp.dot(
-        stacked_ref[...].astype(jnp.bfloat16), inverse_ref[...], preferred_element_type=jnp.float32
-    )
-    out_ref[...] = (terms * norm).reshape(out_ref.shape)
-
-
 def local(nf, nt, nq, strain_rate):
     _, chans, seg_length = strain_rate.shape
     segs = nf * nt
     block = chans // nf
     rows = block + OFFS
     share = OFFS // (nt * nq)
-    group = 4
+    norm = 1.0 / math.sqrt(segs * FREQS)
     vmem = pl.BlockSpec(memory_space=pltpu.VMEM)
-    stacked = pl.pallas_call(
-        functools.partial(stack_kernel, nf, nt, nq),
-        out_shape=jax.ShapeDtypeStruct((share * block, 2 * FREQS), jnp.float32),
+    return pl.pallas_call(
+        functools.partial(stack_kernel, nf, nt, nq, norm),
+        out_shape=jax.ShapeDtypeStruct((share, block, LAGS), jnp.float32),
         in_specs=[pl.BlockSpec(memory_space=pltpu.HBM)] * 2,
         out_specs=vmem,
         scratch_shapes=[
+            pltpu.VMEM((share * block, 2 * FREQS), jnp.float32),
             pltpu.VMEM((chans, seg_length), jnp.bfloat16),
             pltpu.VMEM((seg_length, 2 * FREQS), jnp.bfloat16),
+            pltpu.VMEM((2 * FREQS, 2 * FREQS), jnp.bfloat16),
             pltpu.VMEM((2, chans + OFFS, 2 * LANES), jnp.bfloat16),
             pltpu.VMEM((segs, 2, rows, 2 * LANES), jnp.bfloat16),
             pltpu.VMEM((math.gcd(nf, 4), 4, rows, LANES), jnp.float32),
-            pltpu.SemaphoreType.DMA((4 + chans // 128,)),
+            pltpu.SemaphoreType.DMA((5 + chans // 128,)),
             pltpu.SemaphoreType.DMA((nf, 2)),
             pltpu.SemaphoreType.DMA((nf, nt, 2)),
             pltpu.SemaphoreType.DMA((segs, 2)),
@@ -308,21 +328,9 @@
             pltpu.SemaphoreType.DMA((segs,)),
         ],
         compiler_params=pltpu.CompilerParams(
-            collective_id=0, has_side_effects=True, vmem_limit_bytes=60 << 20
+            collective_id=0, has_side_effects=True, vmem_limit_bytes=50 << 20
         ),
-    )(strain_rate, jnp.asarray(forward_table(seg_length)))
-    norm = 1.0 / math.sqrt(segs * FREQS)
-    return pl.pallas_call(
-        functools.partial(lag_kernel, norm),
-        grid=(share // group,),
-        out_shape=jax.ShapeDtypeStruct((share, block, LAGS), jnp.float32),
-        in_specs=[
-            pl.BlockSpec((group * block, 2 * FREQS), lambda i: (i, 0)),
-            pl.BlockSpec((2 * FREQS, LAGS), lambda i: (0, 0)),
-        ],
-        out_specs=pl.BlockSpec((group, block, LAGS), lambda i: (i, 0, 0)),
-        compiler_params=pltpu.CompilerParams(dimension_semantics=("arbitrary",)),
-    )(stacked, jnp.asarray(inverse_table(seg_length)))
+    )(strain_rate, jnp.asarray(tables(seg_length)))
 
 
 def solution(mesh):

time: 25.5 us -> 22.7 us (0.89)
  Pallas kernels: 25.3 us -> 20.1 us
  local copies, waits for them, and re-layouts: 0 us -> 2.36 us
    pallas_call x2 -> x1, Pallas kernels: 25.3 us -> 20.1 us  [local(): pl.pallas_call(functools.partial(stack_kernel, nf, nt, nq, norm), out_sha...]
    unnamed x0 -> x3, local copies, waits for them, and re-layouts: none -> 2.36 us
where the time goes in v4:
time: 22.7 us; the launch traced here: 22.5 us
  Pallas kernels  20.1 us (89%)
  local copies, waits for them, and re-layouts  2.36 us (10%)
    pallas_call x1, Pallas kernels, local(): pl.pallas_call(functools.partial(stack_kernel, nf, nt, nq, norm), out_sha...  20.1 us
    unnamed x3, local copies, waits for them, and re-layouts  2.36 us

profile of v4, /device:TPU:1, one launch (start us, length us, event | category | flops | bytes accessed | tf_op | source)
XLA Modules:
  0.0 22.5 jit_solution(6756235323009504088)
XLA Ops:
  0.0 0.0 copy-start
  0.0 1.0 %copy-done = bf16[1,256,1024]{2,1,0:T(8,128)(2,1)S(1)} copy-done((bf16[1,256,1024]{2,1,0:T(8,128)(2,1)S(1)}, bf16[1,256,1024]{2,1,0:T(8,128)(2,1)}, u32[]{:S(2)}) %copy-start) | copy-done | bytes 524312
  1.0 20.1 %shard_map.28 = f32[16,64,401]{2,1,0:T(8,128)S(1)} custom-call(bf16[1,256,1024]{2,1,0:T(8,128)(2,1)S(1)} %copy-done, bf16[6144,512]{1,0:T(8,128)(2,1)} %constant.2.clone.table_hbm), custom_call_target="tpu_custom_call" | custom-call | tf_op jit(solution)/shard_map/pallas_call | solution.py:310
  21.2 1.3 %copy.4 = f32[16,64,401]{2,1,0:T(8,128)} copy(f32[16,64,401]{2,1,0:T(8,128)S(1)} %shard_map.28) | data formatting | bytes 3284992
Async XLA Ops:
  0.0 1.0 %copy-start = (bf16[1,256,1024]{2,1,0:T(8,128)(2,1)S(1)}, bf16[1,256,1024]{2,1,0:T(8,128)(2,1)}, u32[]{:S(2)}) copy-start(bf16[1,256,1024]{2,1,0:T(8,128)(2,1)} %x_hbm.1) | copy-start | bytes 1572868

commit v5 on v4

--- a/solution.py
+++ b/solution.py
@@ -218,10 +218,15 @@
         for i in range(1, nt):
             along_tm(fibre, i, c, own=True).start()
 
-    @nearest_first
-    def _(f):
-        for c in range(chunks):
-            along_fibre(f, c).start()
+    def send_rows(d):
+        for f in (fibre + d, fibre - d):
+
+            @pl.when(jnp.logical_and(f >= 0, f < nf))
+            def _(f=f):
+                for c in range(chunks):
+                    along_fibre(f, c).start()
+
+    loop(1, nf, lambda i: send_rows(nf - i))
 
     g_ref[me] = jnp.stack(
         [white[h, pl.ds(pl.multiple_of(fibre * block, 16), rows), :] for h in range(2)]

time: 22.7 us -> 22 us (0.969)
  Pallas kernels: 20.1 us -> 19.5 us
    pallas_call x1, Pallas kernels: 20.1 us -> 19.5 us  [local(): pl.pallas_call(functools.partial(stack_kernel, nf, nt, nq, norm), out_sha...]
where the time goes in v5:
time: 22 us; the launch traced here: 21.8 us
  Pallas kernels  19.5 us (89%)
  local copies, waits for them, and re-layouts  2.36 us (11%)
    pallas_call x1, Pallas kernels, local(): pl.pallas_call(functools.partial(stack_kernel, nf, nt, nq, norm), out_sha...  19.5 us
    unnamed x3, local copies, waits for them, and re-layouts  2.36 us

profile of v5, /device:TPU:1, one launch (start us, length us, event | category | flops | bytes accessed | tf_op | source)
XLA Modules:
  0.0 21.8 jit_solution(17433092242563439598)
XLA Ops:
  0.0 0.0 copy-start
  0.0 1.0 %copy-done = bf16[1,256,1024]{2,1,0:T(8,128)(2,1)S(1)} copy-done((bf16[1,256,1024]{2,1,0:T(8,128)(2,1)S(1)}, bf16[1,256,1024]{2,1,0:T(8,128)(2,1)}, u32[]{:S(2)}) %copy-start) | copy-done | bytes 524312
  1.0 19.5 %shard_map.28 = f32[16,64,401]{2,1,0:T(8,128)S(1)} custom-call(bf16[1,256,1024]{2,1,0:T(8,128)(2,1)S(1)} %copy-done, bf16[6144,512]{1,0:T(8,128)(2,1)} %constant.2.clone.table_hbm), custom_call_target="tpu_custom_call" | custom-call | tf_op jit(solution)/shard_map/pallas_call | solution.py:315
  20.5 1.3 %copy.4 = f32[16,64,401]{2,1,0:T(8,128)} copy(f32[16,64,401]{2,1,0:T(8,128)S(1)} %shard_map.28) | data formatting | bytes 3284992
Async XLA Ops:
  0.0 1.0 %copy-start = (bf16[1,256,1024]{2,1,0:T(8,128)(2,1)S(1)}, bf16[1,256,1024]{2,1,0:T(8,128)(2,1)}, u32[]{:S(2)}) copy-start(bf16[1,256,1024]{2,1,0:T(8,128)(2,1)} %x_hbm.1) | copy-start | bytes 1572868

commit v6 on v5

--- a/solution.py
+++ b/solution.py
@@ -98,7 +98,7 @@
     chans = x_ref.shape[0]
     block = chans // nf
     rows = block + OFFS
-    chunks = 2
+    chunks = 4
     part = rows // chunks
     step = 128
     steps = chans // step
@@ -326,9 +326,9 @@
             pltpu.VMEM((segs, 2, rows, 2 * LANES), jnp.bfloat16),
             pltpu.VMEM((math.gcd(nf, 4), 4, rows, LANES), jnp.float32),
             pltpu.SemaphoreType.DMA((5 + chans // 128,)),
-            pltpu.SemaphoreType.DMA((nf, 2)),
-            pltpu.SemaphoreType.DMA((nf, nt, 2)),
-            pltpu.SemaphoreType.DMA((segs, 2)),
+            pltpu.SemaphoreType.DMA((nf, 4)),
+            pltpu.SemaphoreType.DMA((nf, nt, 4)),
+            pltpu.SemaphoreType.DMA((segs, 4)),
             pltpu.SemaphoreType.DMA((segs,)),
             pltpu.SemaphoreType.DMA((segs,)),
         ],

time: 22 us -> 22.3 us (1.014)
    pallas_call x1, Pallas kernels: 19.5 us -> 19.7 us  [local(): pl.pallas_call(functools.partial(stack_kernel, nf, nt, nq, norm), out_sha...]
where the time goes in v6:
time: 22.3 us; the launch traced here: 22.1 us
  Pallas kernels  19.7 us (88%)
  local copies, waits for them, and re-layouts  2.36 us (11%)
    pallas_call x1, Pallas kernels, local(): pl.pallas_call(functools.partial(stack_kernel, nf, nt, nq, norm), out_sha...  19.7 us
    unnamed x3, local copies, waits for them, and re-layouts  2.36 us

profile of v6, /device:TPU:1, one launch (start us, length us, event | category | flops | bytes accessed | tf_op | source)
XLA Modules:
  0.0 22.1 jit_solution(1302479227790969444)
XLA Ops:
  0.0 0.0 copy-start
  0.0 1.0 %copy-done = bf16[1,256,1024]{2,1,0:T(8,128)(2,1)S(1)} copy-done((bf16[1,256,1024]{2,1,0:T(8,128)(2,1)S(1)}, bf16[1,256,1024]{2,1,0:T(8,128)(2,1)}, u32[]{:S(2)}) %copy-start) | copy-done | bytes 524312
  1.0 19.7 %shard_map.28 = f32[16,64,401]{2,1,0:T(8,128)S(1)} custom-call(bf16[1,256,1024]{2,1,0:T(8,128)(2,1)S(1)} %copy-done, bf16[6144,512]{1,0:T(8,128)(2,1)} %constant.2.clone.table_hbm), custom_call_target="tpu_custom_call" | custom-call | tf_op jit(solution)/shard_map/pallas_call | solution.py:315
  20.8 1.3 %copy.4 = f32[16,64,401]{2,1,0:T(8,128)} copy(f32[16,64,401]{2,1,0:T(8,128)S(1)} %shard_map.28) | data formatting | bytes 3284992
Async XLA Ops:
  0.0 1.0 %copy-start = (bf16[1,256,1024]{2,1,0:T(8,128)(2,1)S(1)}, bf16[1,256,1024]{2,1,0:T(8,128)(2,1)}, u32[]{:S(2)}) copy-start(bf16[1,256,1024]{2,1,0:T(8,128)(2,1)} %x_hbm.1) | copy-start | bytes 1572868
